TPU v7x, 256 devices: a whole 4x4x8 slice. The times are simulated.
256 devices in a mesh: dp: 8 (over z), expert: 32 (over x, y, core).
Axes of the slice: x: 4, y: 4, z: 8, core: 2. Of those that a mesh axis runs over, the one named last changes fastest.
Arguments:
- tokens: bfloat16 [2048, 7168], P('expert', 'dp'), may hold values from -6 to 6
- tangent: bfloat16 [2048, 7168], P('expert', 'dp'), may hold values from -6 to 6
- cotangent: bfloat16 [2048, 7168], P('expert', 'dp'), may hold values from -3 to 3
- routing: int32 [2048, 8], P('expert'), may hold values from 0 to 31, all different within a row; in each aligned block of 64 rows (0 to 63, 64 to 127, ...) at most 18 rows name the same one
- gate_weights: float32 [2048, 8], P('expert'), may hold values from 0.1 to 0.6
- gate_proj: bfloat16 [32, 7168, 2048], P('expert', 'dp'), may hold values from -0.0625 to 0.0625
- up_proj: bfloat16 [32, 7168, 2048], P('expert', 'dp'), may hold values from -0.0625 to 0.0625
- down_proj: bfloat16 [32, 2048, 7168], P('expert', None, 'dp'), may hold values from -0.125 to 0.125
Outputs:
- hessian_product: float32 [2048, 7168], P('expert', 'dp')
Inputs may be any that keep to these rules, and one draw needn't show every extreme that they name: `routing`: each token names 8 different experts. In each aligned block of 64 tokens (the tokens of one index of expert) no expert is named more than 18 times, a bound that some block reaches.
All inputs are finite; a program needn't handle non-finite values.
Results may differ from a plain program's by a relative error of at most 0.0041.
Values may be sent and summed in bfloat16 or wider, within the bound.
A program may use at most 128 MiB of HBM per device.

v0:
```python
import jax
import jax.numpy as jnp
from jax import lax
from jax.sharding import PartitionSpec as P

TOP = 8


def second_order(pre_gate, pre_up, tangent_gate, tangent_up, back_hidden):
    sigma = jax.nn.sigmoid(pre_gate)
    first_slope = sigma * (1.0 + pre_gate * (1.0 - sigma))
    second_slope = sigma * (1.0 - sigma) * (2.0 + pre_gate * (1.0 - 2.0 * sigma))
    factor_a = back_hidden * (second_slope * tangent_gate * pre_up + first_slope * tangent_up)
    factor_b = back_hidden * first_slope * tangent_gate
    return (factor_a.astype(jnp.bfloat16), factor_b.astype(jnp.bfloat16))


def contract_last(left_rows, right_matrix):
    return lax.dot_general(
        left_rows, right_matrix, (((1,), (1,)), ((), ())), preferred_element_type=jnp.float32
    )


def shards(tokens, tangent, cotangent, routing, gate_weights, gate_proj, up_proj, down_proj):
    expert_count = lax.axis_size("expert")
    tok_rows = tokens.shape[0]
    feat_cols = tokens.shape[1]
    capacity = min(tok_rows, tok_rows * TOP // expert_count * 9 // 8)
    slot_total = expert_count * capacity
    routed_flat = routing.reshape(-1)
    route_hits = (
        routed_flat[:, None] == jnp.arange(expert_count, dtype=jnp.int32)[None, :]
    ).astype(jnp.int32)
    slot_index = jnp.sum((jnp.cumsum(route_hits, axis=0) - route_hits) * route_hits, axis=1)
    target_row = routed_flat * capacity + slot_index

    def scatter_rows(values):
        spread = jnp.repeat(values, TOP, axis=0)
        zero_buf = jnp.zeros((slot_total, values.shape[1]), values.dtype)
        return zero_buf.at[target_row].set(spread).reshape(expert_count, capacity, values.shape[1])

    x_rows = lax.all_to_all(
        scatter_rows(tokens), "expert", split_axis=0, concat_axis=0, tiled=True
    ).reshape(slot_total, feat_cols)
    paired = jnp.concatenate([tangent, cotangent], axis=1)
    paired_rows = lax.all_to_all(
        scatter_rows(paired), "expert", split_axis=0, concat_axis=0, tiled=True
    ).reshape(slot_total, 2 * feat_cols)
    v_rows = paired_rows[:, :feat_cols]
    c_rows = paired_rows[:, feat_cols:]
    gate_cols = gate_proj[0]
    up_cols = up_proj[0]
    down_rows = down_proj[0]
    part_gate = jnp.dot(x_rows, gate_cols, preferred_element_type=jnp.float32)
    part_up = jnp.dot(x_rows, up_cols, preferred_element_type=jnp.float32)
    part_tgate = jnp.dot(v_rows, gate_cols, preferred_element_type=jnp.float32)
    part_tup = jnp.dot(v_rows, up_cols, preferred_element_type=jnp.float32)
    part_back = contract_last(c_rows, down_rows)
    summed = (
        lax.psum_scatter(part_gate, "dp", scatter_dimension=0, tiled=True),
        lax.psum_scatter(part_up, "dp", scatter_dimension=0, tiled=True),
        lax.psum_scatter(part_tgate, "dp", scatter_dimension=0, tiled=True),
        lax.psum_scatter(part_tup, "dp", scatter_dimension=0, tiled=True),
        lax.psum_scatter(part_back, "dp", scatter_dimension=0, tiled=True),
    )
    factor_a, factor_b = second_order(summed[0], summed[1], summed[2], summed[3], summed[4])
    factors = jnp.stack([factor_a, factor_b])
    piece = lax.all_gather(factors, "dp", axis=1, tiled=True)
    result_rows = contract_last(piece[0], gate_cols) + contract_last(piece[1], up_cols)
    outgoing = result_rows.astype(jnp.bfloat16).reshape(expert_count, capacity, feat_cols)
    returned = lax.all_to_all(outgoing, "expert", split_axis=0, concat_axis=0, tiled=True).reshape(
        slot_total, feat_cols
    )
    gathered = returned[target_row].reshape(tok_rows, TOP, feat_cols).astype(jnp.float32)
    return jnp.sum(gate_weights[:, :, None] * gathered, axis=1)


def solution(mesh):
    in_specs = (
        P("expert", "dp"),
        P("expert", "dp"),
        P("expert", "dp"),
        P("expert", None),
        P("expert", None),
        P("expert", "dp", None),
        P("expert", "dp", None),
        P("expert", None, "dp"),
    )
    out_specs = P("expert", "dp")
    return jax.shard_map(shards, mesh=mesh, in_specs=in_specs, out_specs=out_specs, check_vma=False)
```

profile of v0, /device:TPU:1, one launch (start us, length us, event | category | flops | bytes accessed | tf_op | source)
XLA Modules:
  0.0 463.8 jit_solution(245255507557251218)
XLA Ops:
  6.5 0.8 copy.12
  7.5 0.7 broadcast_multiply_fusion
  8.2 1.2 reduce-window.6
  10.0 3.0 scatter_custom_fusion.1
  12.9 0.3 reshape.79
  13.3 29.3 %all_to_all.15 = bf16[32,18,896]{2,1,0:T(8,128)(2,1)S(1)} all-to-all(bf16[32,18,896]{2,1,0:T(8,128)(2,1)S(1)} %reshape.79), channel_id=1, replica_groups=mesh['dp'=8,'expert'=32] {'expert'}, dimensions={0} | all-to-all | bytes 2064384 | tf_op jit(solution)/shard_map/all_to_all | solution.py:42
  42.6 0.3 reshape.80
  42.9 6.3 %fusion.4 = f32[576,2048]{1,0:T(8,128)} fusion(bf16[576,896]{1,0:T(8,128)(2,1)S(1)} %reshape.80, bf16[1,896,2048]{2,1,0:T(8,128)(2,1)} %param.14), kind=kOutput, calls=%fused_computation.7 | convolution fusion | flops 2113929216 | bytes 9420800 | tf_op jit(solution)/shard_map/dot_general | solution.py:55
  49.3 6.3 %fusion.10 = f32[576,2048]{1,0:T(8,128)} fusion(bf16[576,896]{1,0:T(8,128)(2,1)S(1)} %reshape.80, bf16[1,896,2048]{2,1,0:T(8,128)(2,1)} %param.13), kind=kOutput, calls=%fused_computation.13 | convolution fusion | flops 2113929216 | bytes 9420800 | tf_op jit(solution)/shard_map/dot_general | solution.py:54
  55.7 0.8 copy-done.1
  56.6 4.8 %scatter_custom_fusion = bf16[576,1792]{1,0:T(8,128)(2,1)} fusion(s32[512]{0:T(512)S(1)} %bitcast.64, bf16[]{:T(256)} %constant.7.clone.1, bf16[64,1792]{1,0:T(8,128)(2,1)S(1)} %pad_maximum_fusion.1), kind=kCustom, calls=%fused_computation.22 | custom fusion | bytes 2293762 | tf_op jit(solution)/shard_map/scatter | solution.py:40
  61.4 2.6 reshape.76
  64.0 39.1 %all_to_all.16 = bf16[32,18,1792]{2,1,0:T(8,128)(2,1)} all-to-all(bf16[32,18,1792]{2,1,0:T(8,128)(2,1)S(1)} %reshape.76), channel_id=1, replica_groups=mesh['dp'=8,'expert'=32] {'expert'}, dimensions={0} | all-to-all | bytes 4128768 | tf_op jit(solution)/shard_map/all_to_all | solution.py:46
  103.1 2.8 reshape.77
  105.9 6.4 %fusion.8 = f32[576,2048]{1,0:T(8,128)} fusion(bf16[1,896,2048]{2,1,0:T(8,128)(2,1)} %param.13, bf16[576,1792]{1,0:T(8,128)(2,1)S(1)} %reshape.77), kind=kOutput, calls=%fused_computation.11 | convolution fusion | flops 2113929216 | bytes 9420800 | tf_op jit(solution)/shard_map/dot_general | solution.py:56
  112.6 6.3 %fusion.2 = f32[576,2048]{1,0:T(8,128)} fusion(bf16[1,896,2048]{2,1,0:T(8,128)(2,1)} %param.14, bf16[576,1792]{1,0:T(8,128)(2,1)S(1)} %reshape.77), kind=kOutput, calls=%fused_computation.5 | convolution fusion | flops 2113929216 | bytes 9420800 | tf_op jit(solution)/shard_map/dot_general | solution.py:57
  118.9 6.4 %fusion.12 = f32[576,2048]{1,0:T(8,128)} fusion(bf16[1,2048,896]{2,1,0:T(8,128)(2,1)} %param.15, bf16[576,1792]{1,0:T(8,128)(2,1)S(1)} %reshape.77), kind=kOutput, calls=%fused_computation.15 | convolution fusion | flops 2113929216 | bytes 9420800 | tf_op jit(solution)/shard_map/dot_general | solution.py:19
  125.4 44.6 %reduce-scatter.8.cloned.1.call-done = f32[72,2048]{1,0:T(8,128)} async-done(((f32[576,2048]{1,0:T(8,128)}), f32[72,2048]{1,0:T(8,128)}) %reduce-scatter.8.cloned.1.call-update) | async-done | bytes 589840 | tf_op jit(solution)/shard_map/reduce_scatter | solution.py:60
  170.0 61.5 %reduce-scatter.10.cloned.1.call-done = f32[72,2048]{1,0:T(8,128)} async-done(((f32[576,2048]{1,0:T(8,128)}), f32[72,2048]{1,0:T(8,128)}) %reduce-scatter.10.cloned.1.call-update) | async-done | bytes 589840 | tf_op jit(solution)/shard_map/reduce_scatter | solution.py:62
  231.5 61.3 %reduce-scatter.14.cloned.1.call-done = f32[72,2048]{1,0:T(8,128)} async-done(((f32[576,2048]{1,0:T(8,128)}), f32[72,2048]{1,0:T(8,128)}) %reduce-scatter.14.cloned.1.call-update) | async-done | bytes 589840 | tf_op jit(solution)/shard_map/reduce_scatter | solution.py:63
  292.8 61.3 %reduce-scatter.6.cloned.1.call-done = f32[72,2048]{1,0:T(8,128)} async-done(((f32[576,2048]{1,0:T(8,128)}), f32[72,2048]{1,0:T(8,128)}) %reduce-scatter.6.cloned.1.call-update) | async-done | bytes 589840 | tf_op jit(solution)/shard_map/reduce_scatter | solution.py:64
  354.1 2.2 fusion.37
  356.3 0.9 pad_maximum_fusion
  357.2 58.5 %all-gather.2.cloned.1.call-done = bf16[2,576,2048]{2,1,0:T(8,128)(2,1)} async-done(((bf16[2,72,2048]{2,1,0:T(8,128)(2,1)}), bf16[2,576,2048]{2,1,0:T(8,128)(2,1)}) %all-gather.2.cloned.1.call-update) | async-done | bytes 4718608 | tf_op jit(solution)/shard_map/all_gather | solution.py:68
  415.7 5.5 %fusion = f32[576,896]{1,0:T(8,128)S(1)} fusion(bf16[1,896,2048]{2,1,0:T(8,128)(2,1)} %param.14, bf16[2,576,2048]{2,1,0:T(8,128)(2,1)} %all-gather.2.cloned.1.call-done), kind=kOutput, calls=%fused_computation.3 | convolution fusion | flops 2113929216 | bytes 8093696 | tf_op jit(solution)/shard_map/dot_general | solution.py:19
  421.3 2.7 add_convert_fusion
  423.9 1.3 reshape.81
  425.2 7.5 %all-to-all-start.2 = ((bf16[32,18,896]{2,1,0:T(8,128)(2,1)}), bf16[32,18,896]{2,1,0:T(8,128)(2,1)S(1)}, u32[]{:S(2)}, u32[]{:S(2)}) async-start(bf16[32,18,896]{2,1,0:T(8,128)(2,1)} %reshape.81), calls=%async_computation.7 | async-start | bytes 2752512 | tf_op jit(solution)/shard_map/all_to_all | solution.py:71
  432.8 20.4 %all-to-all-done.2 = bf16[32,18,896]{2,1,0:T(8,128)(2,1)S(1)} async-done(((bf16[32,18,896]{2,1,0:T(8,128)(2,1)}), bf16[32,18,896]{2,1,0:T(8,128)(2,1)S(1)}, u32[]{:S(2)}, u32[]{:S(2)}) %all-to-all-start.2) | async-done | bytes 1032224 | tf_op jit(solution)/shard_map/all_to_all | solution.py:71
  453.2 0.3 reshape.82
  453.6 2.1 gather_fusion
  455.6 1.3 fusion.14
  (37 shorter events, 1.4 us)
Async XLA Ops:
  6.5 3.4 copy-start
  6.5 118.8 %reduce-scatter.12.cloned.1.call-start = ((), (), s32[]{:S(2)}) async-start(), calls=%async_computation.11 | async-start | bytes 5308416 | tf_op jit(solution)/shard_map/reduce_scatter | solution.py:61
  49.2 120.8 %reduce-scatter.8.cloned.1.call-start = ((), (), s32[]{:S(2)}) async-start(), calls=%async_computation.9 | async-start | bytes 5308416 | tf_op jit(solution)/shard_map/reduce_scatter | solution.py:60
  55.6 0.9 copy-start.1
  55.6 1.0 copy-start.2
  55.6 175.8 %reduce-scatter.10.cloned.1.call-start = ((), (), s32[]{:S(2)}) async-start(), calls=%async_computation.10 | async-start | bytes 5308416 | tf_op jit(solution)/shard_map/reduce_scatter | solution.py:62
  112.3 180.5 %reduce-scatter.14.cloned.1.call-start = ((), (), s32[]{:S(2)}) async-start(), calls=%async_computation.12 | async-start | bytes 5308416 | tf_op jit(solution)/shard_map/reduce_scatter | solution.py:63
  118.9 235.2 %reduce-scatter.6.cloned.1.call-start = ((), (), s32[]{:S(2)}) async-start(), calls=%async_computation.8 | async-start | bytes 5308416 | tf_op jit(solution)/shard_map/reduce_scatter | solution.py:64
  125.3 290.4 %all-gather.2.cloned.1.call-start = ((), (), s32[]{:S(2)}) async-start(), calls=%async_computation.13 | async-start | bytes 5308416 | tf_op jit(solution)/shard_map/all_gather | solution.py:68
  415.7 5.5 %copy-start.4 = (bf16[2,576,2048]{2,1,0:T(8,128)(2,1)S(1)}, bf16[2,576,2048]{2,1,0:T(8,128)(2,1)}, u32[]{:S(2)}) copy-start(bf16[2,576,2048]{2,1,0:T(8,128)(2,1)} %all-gather.2.cloned.1.call-done) | copy-start | bytes 14155780
  415.7 5.5 %copy-start.5 = (bf16[1,896,2048]{2,1,0:T(8,128)(2,1)S(1)}, bf16[1,896,2048]{2,1,0:T(8,128)(2,1)}, u32[]{:S(2)}) copy-start(bf16[1,896,2048]{2,1,0:T(8,128)(2,1)} %param.13) | copy-start | bytes 11010052
  423.9 8.8 %copy-start.3 = (f32[64,8]{0,1:T(8,128)S(1)}, f32[64,8]{0,1:T(8,128)}, u32[]{:S(2)}) copy-start(f32[64,8]{0,1:T(8,128)} %param.12) | copy-start | bytes 6148
  425.2 28.0 %all-to-all-start.2 = ((bf16[32,18,896]{2,1,0:T(8,128)(2,1)}), bf16[32,18,896]{2,1,0:T(8,128)(2,1)S(1)}, u32[]{:S(2)}, u32[]{:S(2)}) async-start(bf16[32,18,896]{2,1,0:T(8,128)(2,1)} %reshape.81), calls=%async_computation.7 | async-start | bytes 2752512 | tf_op jit(solution)/shard_map/all_to_all | solution.py:71
Sparse Core Ops, SparseCore 0:
  49.3 59.1 reduce-scatter.11
  111.0 58.8 reduce-scatter.7
  172.5 58.8 reduce-scatter.9
  233.9 58.8 reduce-scatter.13
  295.2 58.8 reduce-scatter.5
  357.3 58.3 all-gather.1
where the time goes:
time: 464 us
  waiting for transfers between devices  308 us (66%)
  blocking collectives  68.4 us (15%)
  matrix products  39.8 us (9%)
  local copies, waits for them, and re-layouts  19.9 us (4%)
  between operations  13.6 us (3%)
  starting transfers between devices  7.92 us (2%)
  other arithmetic  6.42 us (1%)
    reduce_scatter x1, waiting for transfers between devices, shards(): lax.psum_scatter(part_tgate, 'dp', scatter_dimension=0, tiled=True)  61.5 us
    reduce_scatter x1, waiting for transfers between devices, shards(): lax.psum_scatter(part_tup, 'dp', scatter_dimension=0, tiled=True)  61.3 us
    reduce_scatter x1, waiting for transfers between devices, shards(): lax.psum_scatter(part_back, 'dp', scatter_dimension=0, tiled=True)  61.3 us
    all_gather x1, waiting for transfers between devices, shards(): piece = lax.all_gather(factors, 'dp', axis=1, tiled=True)  58.5 us
    reduce_scatter x1, waiting for transfers between devices, shards(): lax.psum_scatter(part_gate, 'dp', scatter_dimension=0, tiled=True)  44.6 us
    all_to_all x1, blocking collectives, shards(): lax.all_to_all(scatter_rows(paired), 'expert', split_axis=0, concat_axis=...  39.1 us
    all_to_all x1, blocking collectives, shards(): lax.all_to_all(scatter_rows(tokens), 'expert', split_axis=0, concat_axis=...  29.3 us
    all_to_all x1, waiting for transfers between devices, shards(): lax.all_to_all(outgoing, 'expert', split_axis=0, concat_axis=0, tiled=True)  20.4 us
  transfers between devices with their start and end apart: 7, of which 6 were waited for; matrix products, arithmetic and copies ran while one was open for 8% of the time, Pallas kernels for 0%

commit v1 on v0

--- a/solution.py
+++ b/solution.py
@@ -4,6 +4,29 @@
 from jax.sharding import PartitionSpec as P
 
 TOP = 8
+
+
+def _move_task(inp):
+    block_out = jax.lax.axis_size("dp")
+    seen_now = jax.lax.axis_index("dp")
+    finding, state_now, step_out = (block_out, seen_now, inp.shape[1])
+    nodes = tuple((pp * finding if b == 1 else pp for b, pp in enumerate(inp.shape)))
+    wide_out = jnp.zeros(nodes, inp.dtype)
+    left_arr = lax.dynamic_update_slice_in_dim(wide_out, inp, state_now * step_out, axis=1)
+    near = back = inp
+    for tick in tuple(range(1, finding // 2 + 1)):
+        then = tuple(((b, (b + 1) % finding) for b in range(finding)))
+        near = jax.lax.ppermute(near, "dp", then)
+        left_arr = lax.dynamic_update_slice_in_dim(
+            left_arr, near, (state_now - tick) % finding * step_out, axis=1
+        )
+        if 2 * tick < finding:
+            front = tuple(((b, (b - 1) % finding) for b in range(finding)))
+            back = jax.lax.ppermute(back, "dp", front)
+            left_arr = lax.dynamic_update_slice_in_dim(
+                left_arr, back, (state_now + tick) % finding * step_out, axis=1
+            )
+    return left_arr
 
 
 def second_order(pre_gate, pre_up, tangent_gate, tangent_up, back_hidden):
@@ -65,7 +88,7 @@
     )
     factor_a, factor_b = second_order(summed[0], summed[1], summed[2], summed[3], summed[4])
     factors = jnp.stack([factor_a, factor_b])
-    piece = lax.all_gather(factors, "dp", axis=1, tiled=True)
+    piece = _move_task(factors)
     result_rows = contract_last(piece[0], gate_cols) + contract_last(piece[1], up_cols)
     outgoing = result_rows.astype(jnp.bfloat16).reshape(expert_count, capacity, feat_cols)
     returned = lax.all_to_all(outgoing, "expert", split_axis=0, concat_axis=0, tiled=True).reshape(

time: 464 us -> 470 us (1.013)
  waiting for transfers between devices: 308 us -> 292 us
  starting transfers between devices: 7.92 us -> 19.5 us
  local copies, waits for them, and re-layouts: 19.9 us -> 28.6 us
    all_gather x1 -> x0, waiting for transfers between devices: 58.5 us -> none  [shards(): piece = lax.all_gather(factors, 'dp', axis=1, tiled=True)]
    ppermute x0 -> x7, waiting for transfers between devices: none -> 43.1 us  [the longest x4 43.1 us: _move_task(): near = jax.lax.ppermute(near, 'dp', then)]
    ppermute x0 -> x7, starting transfers between devices: none -> 8 us  [the longest x3 7.99 us: _move_task(): back = jax.lax.ppermute(back, 'dp', front)]
    dynamic_update_slice x0 -> x7, local copies, waits for them, and re-layouts: none -> 6.04 us  [the longest x4 3.43 us: _move_task(): lax.dynamic_update_slice_in_dim(left_arr, near, (state_now - tick) % find...]
  transfers between devices with their start and end apart: 7 -> 13, of which waited for: 6 -> 9; matrix products, arithmetic and copies ran while one was open for 8% -> 9% of each run, Pallas kernels for 0% -> 0%
where the time goes in v1:
time: 470 us; the launch traced here: 469 us
  waiting for transfers between devices  292 us (62%)
  blocking collectives  68.4 us (15%)
  matrix products  40.4 us (9%)
  local copies, waits for them, and re-layouts  28.6 us (6%)
  starting transfers between devices  19.5 us (4%)
  between operations  13.3 us (3%)
  other arithmetic  6.52 us (1%)
    reduce_scatter x1, waiting for transfers between devices, shards(): lax.psum_scatter(part_back, 'dp', scatter_dimension=0, tiled=True)  61.5 us
    reduce_scatter x1, waiting for transfers between devices, shards(): lax.psum_scatter(part_tup, 'dp', scatter_dimension=0, tiled=True)  61.3 us
    reduce_scatter x1, waiting for transfers between devices, shards(): lax.psum_scatter(part_tgate, 'dp', scatter_dimension=0, tiled=True)  61.3 us
    reduce_scatter x1, waiting for transfers between devices, shards(): lax.psum_scatter(part_gate, 'dp', scatter_dimension=0, tiled=True)  44.6 us
    ppermute x4, waiting for transfers between devices, _move_task(): near = jax.lax.ppermute(near, 'dp', then)  43.1 us
    all_to_all x1, blocking collectives, shards(): lax.all_to_all(scatter_rows(paired), 'expert', split_axis=0, concat_axis=...  39.1 us
    all_to_all x1, blocking collectives, shards(): lax.all_to_all(scatter_rows(tokens), 'expert', split_axis=0, concat_axis=...  29.3 us
    all_to_all x1, waiting for transfers between devices, shards(): lax.all_to_all(outgoing, 'expert', split_axis=0, concat_axis=0, tiled=True)  20.4 us
  transfers between devices with their start and end apart: 13, of which 9 were waited for; matrix products, arithmetic and copies ran while one was open for 9% of the time, Pallas kernels for 0%

profile of v1, /device:TPU:1, one launch (start us, length us, event | category | flops | bytes accessed | tf_op | source)
XLA Modules:
  0.0 469.1 jit_solution(16771063360271546530)
XLA Ops:
  8.4 1.2 reduce-window.6
  10.0 3.0 scatter_custom_fusion.1
  13.3 29.3 %all_to_all.15 = bf16[32,18,896]{2,1,0:T(8,128)(2,1)S(1)} all-to-all(bf16[32,18,896]{2,1,0:T(8,128)(2,1)S(1)} %reshape.79), channel_id=1, replica_groups=mesh['dp'=8,'expert'=32] {'expert'}, dimensions={0} | all-to-all | bytes 2064384 | tf_op jit(solution)/shard_map/all_to_all | solution.py:65
  42.9 6.3 %fusion.4 = f32[576,2048]{1,0:T(8,128)} fusion(bf16[576,896]{1,0:T(8,128)(2,1)S(1)} %reshape.80, bf16[1,896,2048]{2,1,0:T(8,128)(2,1)} %param.14), kind=kOutput, calls=%fused_computation.7 | convolution fusion | flops 2113929216 | bytes 9420800 | tf_op jit(solution)/shard_map/dot_general | solution.py:78
  49.3 6.3 %fusion.10 = f32[576,2048]{1,0:T(8,128)} fusion(bf16[576,896]{1,0:T(8,128)(2,1)S(1)} %reshape.80, bf16[1,896,2048]{2,1,0:T(8,128)(2,1)} %param.13), kind=kOutput, calls=%fused_computation.13 | convolution fusion | flops 2113929216 | bytes 9420800 | tf_op jit(solution)/shard_map/dot_general | solution.py:77
  56.6 4.8 %scatter_custom_fusion = bf16[576,1792]{1,0:T(8,128)(2,1)} fusion(s32[512]{0:T(512)S(1)} %bitcast.64, bf16[]{:T(256)} %constant.62.clone.1, bf16[64,1792]{1,0:T(8,128)(2,1)S(1)} %pad_maximum_fusion.1), kind=kCustom, calls=%fused_computation.22 | custom fusion | bytes 2293762 | tf_op jit(solution)/shard_map/scatter | solution.py:63
  61.4 2.6 reshape.76
  64.0 39.1 %all_to_all.16 = bf16[32,18,1792]{2,1,0:T(8,128)(2,1)} all-to-all(bf16[32,18,1792]{2,1,0:T(8,128)(2,1)S(1)} %reshape.76), channel_id=1, replica_groups=mesh['dp'=8,'expert'=32] {'expert'}, dimensions={0} | all-to-all | bytes 4128768 | tf_op jit(solution)/shard_map/all_to_all | solution.py:69
  103.1 2.8 reshape.77
  105.9 6.5 %fusion.12 = f32[576,2048]{1,0:T(8,128)} fusion(bf16[1,2048,896]{2,1,0:T(8,128)(2,1)} %param.15, bf16[576,1792]{1,0:T(8,128)(2,1)S(1)} %reshape.77), kind=kOutput, calls=%fused_computation.15 | convolution fusion | flops 2113929216 | bytes 9420800 | tf_op jit(solution)/shard_map/dot_general | solution.py:42
  112.7 6.3 %fusion.2 = f32[576,2048]{1,0:T(8,128)} fusion(bf16[1,896,2048]{2,1,0:T(8,128)(2,1)} %param.14, bf16[576,1792]{1,0:T(8,128)(2,1)S(1)} %reshape.77), kind=kOutput, calls=%fused_computation.5 | convolution fusion | flops 2113929216 | bytes 9420800 | tf_op jit(solution)/shard_map/dot_general | solution.py:80
  119.0 6.3 %fusion.8 = f32[576,2048]{1,0:T(8,128)} fusion(bf16[1,896,2048]{2,1,0:T(8,128)(2,1)} %param.13, bf16[576,1792]{1,0:T(8,128)(2,1)S(1)} %reshape.77), kind=kOutput, calls=%fused_computation.11 | convolution fusion | flops 2113929216 | bytes 9420800 | tf_op jit(solution)/shard_map/dot_general | solution.py:79
  125.4 44.6 %reduce-scatter.8.cloned.1.call-done = f32[72,2048]{1,0:T(8,128)} async-done(((f32[576,2048]{1,0:T(8,128)}), f32[72,2048]{1,0:T(8,128)}) %reduce-scatter.8.cloned.1.call-update) | async-done | bytes 589840 | tf_op jit(solution)/shard_map/reduce_scatter | solution.py:83
  169.9 61.5 %reduce-scatter.6.cloned.1.call-done = f32[72,2048]{1,0:T(8,128)} async-done(((f32[576,2048]{1,0:T(8,128)}), f32[72,2048]{1,0:T(8,128)}) %reduce-scatter.6.cloned.1.call-update) | async-done | bytes 589840 | tf_op jit(solution)/shard_map/reduce_scatter | solution.py:87
  231.4 61.3 %reduce-scatter.14.cloned.1.call-done = f32[72,2048]{1,0:T(8,128)} async-done(((f32[576,2048]{1,0:T(8,128)}), f32[72,2048]{1,0:T(8,128)}) %reduce-scatter.14.cloned.1.call-update) | async-done | bytes 589840 | tf_op jit(solution)/shard_map/reduce_scatter | solution.py:86
  292.8 61.3 %reduce-scatter.10.cloned.1.call-done = f32[72,2048]{1,0:T(8,128)} async-done(((f32[576,2048]{1,0:T(8,128)}), f32[72,2048]{1,0:T(8,128)}) %reduce-scatter.10.cloned.1.call-update) | async-done | bytes 589840 | tf_op jit(solution)/shard_map/reduce_scatter | solution.py:85
  354.1 2.2 fusion.37
  356.3 2.7 broadcast_in_dim.20
  360.0 2.7 collective-permute-start.1
  362.7 12.8 %collective-permute-done = bf16[2,72,2048]{2,1,0:T(8,128)(2,1)S(1)} collective-permute-done((bf16[2,72,2048]{2,1,0:T(8,128)(2,1)S(1)}, bf16[2,72,2048]{2,1,0:T(8,128)(2,1)S(1)}, u32[]{:S(2)}, u32[]{:S(2)}) %collective-permute-start) | collective-permute-done | bytes 589856 | tf_op jit(solution)/shard_map/ppermute | solution.py:19
  375.4 2.7 collective-permute-start.3
  378.1 11.9 %collective-permute-done.2 = bf16[2,72,2048]{2,1,0:T(8,128)(2,1)S(1)} collective-permute-done((bf16[2,72,2048]{2,1,0:T(8,128)(2,1)S(1)}, bf16[2,72,2048]{2,1,0:T(8,128)(2,1)S(1)}, u32[]{:S(2)}, u32[]{:S(2)}) %collective-permute-start.2) | collective-permute-done | bytes 589856 | tf_op jit(solution)/shard_map/ppermute | solution.py:19
  391.7 2.6 collective-permute-start.5
  395.2 8.4 %collective-permute-done.4 = bf16[2,72,2048]{2,1,0:T(8,128)(2,1)S(1)} collective-permute-done((bf16[2,72,2048]{2,1,0:T(8,128)(2,1)S(1)}, bf16[2,72,2048]{2,1,0:T(8,128)(2,1)S(1)}, u32[]{:S(2)}, u32[]{:S(2)}) %collective-permute-start.4) | collective-permute-done | bytes 589856 | tf_op jit(solution)/shard_map/ppermute | solution.py:19
  406.2 10.1 %collective-permute-done.6 = bf16[2,72,2048]{2,1,0:T(8,128)(2,1)S(1)} collective-permute-done((bf16[2,72,2048]{2,1,0:T(8,128)(2,1)S(1)}, bf16[2,72,2048]{2,1,0:T(8,128)(2,1)S(1)}, u32[]{:S(2)}, u32[]{:S(2)}) %collective-permute-start.6) | collective-permute-done | bytes 589856 | tf_op jit(solution)/shard_map/ppermute | solution.py:19
  417.2 4.4 fusion
  421.6 4.3 add_convert_fusion
  425.9 1.3 reshape.81
  427.2 11.1 %all-to-all-start.2 = ((bf16[32,18,896]{2,1,0:T(8,128)(2,1)}), bf16[32,18,896]{2,1,0:T(8,128)(2,1)S(1)}, u32[]{:S(2)}, u32[]{:S(2)}) async-start(bf16[32,18,896]{2,1,0:T(8,128)(2,1)} %reshape.81), calls=%async_computation.7 | async-start | bytes 2752512 | tf_op jit(solution)/shard_map/all_to_all | solution.py:94
  438.4 20.4 %all-to-all-done.2 = bf16[32,18,896]{2,1,0:T(8,128)(2,1)S(1)} async-done(((bf16[32,18,896]{2,1,0:T(8,128)(2,1)}), bf16[32,18,896]{2,1,0:T(8,128)(2,1)S(1)}, u32[]{:S(2)}, u32[]{:S(2)}) %all-to-all-start.2) | async-done | bytes 1032224 | tf_op jit(solution)/shard_map/all_to_all | solution.py:94
  459.2 2.1 gather_fusion
  461.3 1.3 fusion.14
  (58 shorter events, 11.7 us)
Async XLA Ops:
  6.5 3.4 copy-start
  6.5 118.8 %reduce-scatter.12.cloned.1.call-start = ((), (), s32[]{:S(2)}) async-start(), calls=%async_computation.11 | async-start | bytes 5308416 | tf_op jit(solution)/shard_map/reduce_scatter | solution.py:84
  49.2 120.7 %reduce-scatter.8.cloned.1.call-start = ((), (), s32[]{:S(2)}) async-start(), calls=%async_computation.9 | async-start | bytes 5308416 | tf_op jit(solution)/shard_map/reduce_scatter | solution.py:83
  55.6 0.9 copy-start.2
  55.6 1.0 copy-start.3
  55.6 175.8 %reduce-scatter.6.cloned.1.call-start = ((), (), s32[]{:S(2)}) async-start(), calls=%async_computation.8 | async-start | bytes 5308416 | tf_op jit(solution)/shard_map/reduce_scatter | solution.py:87
  112.4 180.3 %reduce-scatter.14.cloned.1.call-start = ((), (), s32[]{:S(2)}) async-start(), calls=%async_computation.12 | async-start | bytes 5308416 | tf_op jit(solution)/shard_map/reduce_scatter | solution.py:86
  119.0 235.1 %reduce-scatter.10.cloned.1.call-start = ((), (), s32[]{:S(2)}) async-start(), calls=%async_computation.10 | async-start | bytes 5308416 | tf_op jit(solution)/shard_map/reduce_scatter | solution.py:85
  360.0 15.5 %collective-permute-start = (bf16[2,72,2048]{2,1,0:T(8,128)(2,1)S(1)}, bf16[2,72,2048]{2,1,0:T(8,128)(2,1)S(1)}, u32[]{:S(2)}, u32[]{:S(2)}) collective-permute-start(bf16[2,72,2048]{2,1,0:T(8,128)(2,1)S(1)} %get-tuple-element.7), channel_id=1, source_target_pairs={{0,32},{32,64},{64,96},{96,128},{128,160},{160,192},{192,224},{224... | collective-permute-start | bytes 1769480 | tf_op jit(solution)/shard_map/ppermute | solution.py:19
  360.0 15.5 %collective-permute-start.1 = (bf16[2,72,2048]{2,1,0:T(8,128)(2,1)S(1)}, bf16[2,72,2048]{2,1,0:T(8,128)(2,1)S(1)}, u32[]{:S(2)}, u32[]{:S(2)}) collective-permute-start(bf16[2,72,2048]{2,1,0:T(8,128)(2,1)S(1)} %get-tuple-element.7), channel_id=1, source_target_pairs={{0,224},{32,0},{64,32},{96,64},{128,96},{160,128},{192,160},{224,1... | collective-permute-start | bytes 1769480 | tf_op jit(solution)/shard_map/ppermute | solution.py:25
  375.4 14.5 %collective-permute-start.2 = (bf16[2,72,2048]{2,1,0:T(8,128)(2,1)S(1)}, bf16[2,72,2048]{2,1,0:T(8,128)(2,1)S(1)}, u32[]{:S(2)}, u32[]{:S(2)}) collective-permute-start(bf16[2,72,2048]{2,1,0:T(8,128)(2,1)S(1)} %collective-permute-done), channel_id=1, source_target_pairs={{0,32},{32,64},{64,96},{96,128},{128,160},{160,192},{192,224},{224... | collective-permute-start | bytes 1769480 | tf_op jit(solution)/shard_map/ppermute | solution.py:19
  375.4 16.3 %collective-permute-start.3 = (bf16[2,72,2048]{2,1,0:T(8,128)(2,1)S(1)}, bf16[2,72,2048]{2,1,0:T(8,128)(2,1)S(1)}, u32[]{:S(2)}, u32[]{:S(2)}) collective-permute-start(bf16[2,72,2048]{2,1,0:T(8,128)(2,1)S(1)} %collective-permute-done.1), channel_id=1, source_target_pairs={{0,224},{32,0},{64,32},{96,64},{128,96},{160,128},{192,160},{224,1... | collective-permute-start | bytes 1769480 | tf_op jit(solution)/shard_map/ppermute | solution.py:25
  390.0 13.6 %collective-permute-start.4 = (bf16[2,72,2048]{2,1,0:T(8,128)(2,1)S(1)}, bf16[2,72,2048]{2,1,0:T(8,128)(2,1)S(1)}, u32[]{:S(2)}, u32[]{:S(2)}) collective-permute-start(bf16[2,72,2048]{2,1,0:T(8,128)(2,1)S(1)} %collective-permute-done.2), channel_id=1, source_target_pairs={{0,32},{32,64},{64,96},{96,128},{128,160},{160,192},{192,224},{224... | collective-permute-start | bytes 1769480 | tf_op jit(solution)/shard_map/ppermute | solution.py:19
  390.8 26.3 %copy-start.5 = (bf16[1,896,2048]{2,1,0:T(8,128)(2,1)S(1)}, bf16[1,896,2048]{2,1,0:T(8,128)(2,1)}, u32[]{:S(2)}) copy-start(bf16[1,896,2048]{2,1,0:T(8,128)(2,1)} %param.14) | copy-start | bytes 11010052
  391.7 13.6 %collective-permute-start.5 = (bf16[2,72,2048]{2,1,0:T(8,128)(2,1)S(1)}, bf16[2,72,2048]{2,1,0:T(8,128)(2,1)S(1)}, u32[]{:S(2)}, u32[]{:S(2)}) collective-permute-start(bf16[2,72,2048]{2,1,0:T(8,128)(2,1)S(1)} %collective-permute-done.3), channel_id=1, source_target_pairs={{0,224},{32,0},{64,32},{96,64},{128,96},{160,128},{192,160},{224,1... | collective-permute-start | bytes 1769480 | tf_op jit(solution)/shard_map/ppermute | solution.py:25
  403.6 12.7 %collective-permute-start.6 = (bf16[2,72,2048]{2,1,0:T(8,128)(2,1)S(1)}, bf16[2,72,2048]{2,1,0:T(8,128)(2,1)S(1)}, u32[]{:S(2)}, u32[]{:S(2)}) collective-permute-start(bf16[2,72,2048]{2,1,0:T(8,128)(2,1)S(1)} %collective-permute-done.4), channel_id=1, source_target_pairs={{0,32},{32,64},{64,96},{96,128},{128,160},{160,192},{192,224},{224... | collective-permute-start | bytes 1769480 | tf_op jit(solution)/shard_map/ppermute | solution.py:19
  417.2 4.5 copy-start.6
  425.9 12.4 %copy-start.4 = (f32[64,8]{0,1:T(8,128)S(1)}, f32[64,8]{0,1:T(8,128)}, u32[]{:S(2)}) copy-start(f32[64,8]{0,1:T(8,128)} %param.12) | copy-start | bytes 6148
  427.2 31.6 %all-to-all-start.2 = ((bf16[32,18,896]{2,1,0:T(8,128)(2,1)}), bf16[32,18,896]{2,1,0:T(8,128)(2,1)S(1)}, u32[]{:S(2)}, u32[]{:S(2)}) async-start(bf16[32,18,896]{2,1,0:T(8,128)(2,1)} %reshape.81), calls=%async_computation.7 | async-start | bytes 2752512 | tf_op jit(solution)/shard_map/all_to_all | solution.py:94
  458.8 3.7 copy-start.1
Sparse Core Ops, SparseCore 0:
  49.3 59.1 reduce-scatter.11
  111.0 58.8 reduce-scatter.7
  172.5 58.8 reduce-scatter.5
  233.8 58.8 reduce-scatter.13
  295.2 58.8 reduce-scatter.9
